TPU v7x, 256 devices: a whole 4x4x8 slice. The times are simulated.
256 devices in a mesh: vir: 32 (over x, z), occ: 4 (over y), rep: 2 (over core).
Axes of the slice: x: 4, y: 4, z: 8, core: 2. Of those that a mesh axis runs over, the one named last changes fastest.
Arguments:
- amplitudes: float32 [256, 64, 4096], P('vir', ('occ', 'rep')), may hold values from -6 to 6
- integrals: float32 [384, 512, 4096], P('vir', None, ('occ', 'rep')), may hold values from -0.005859375 to 0.005859375
- block_owner: int32 [256], replicated, may hold values from 0 to 31, as said below
Outputs:
- ladder: float32 [64, 512], P('occ', 'rep')
Inputs may be any that keep to these rules, and one draw needn't show every extreme that they name: `block_owner`: blocks 8 * s to 8 * s + 7 start on vir index s. No vir index owns more than 12 blocks and some owns exactly 12; slots beyond an index's count are unused. No vir index's starting blocks name one owner more than 2 times, and each names some owner exactly 2 times.
All inputs are finite; a program needn't handle non-finite values.
Results may differ from a plain program's by a relative error of at most 0.0001.
Values sent between devices are 32-bit elements; how exact they have to be, the bound alone decides.
No kernel may reach another device: no remote copies, remote signals or barrier semaphores. Data moves between devices by JAX's collectives and lax.ppermute only.
A program may use at most 128 MiB of HBM per device.

v0:
```python
import jax
import jax.numpy as jnp
from jax import lax
from jax.sharding import PartitionSpec as P


def block_ranks(owners, blocks_dev):
    block_ids = jnp.arange(owners.shape[0], dtype=jnp.int32)
    earlier = block_ids[None, :] < block_ids[:, None]
    same_owner = owners[None, :] == owners[:, None]
    same_source = block_ids[None, :] // blocks_dev == block_ids[:, None] // blocks_dev
    owner_rank = jnp.sum(jnp.where(same_owner & earlier, 1, 0), axis=1).astype(jnp.int32)
    src_rank = jnp.sum(jnp.where(same_owner & earlier & same_source, 1, 0), axis=1).astype(
        jnp.int32
    )
    return (owner_rank, src_rank)


def contract(owned, integrals):
    return jnp.einsum(
        "vpx,vax->pa",
        owned,
        integrals,
        precision=lax.Precision.HIGHEST,
        preferred_element_type=jnp.float32,
    )


def on_device(amplitudes, integrals, block_owner):
    vir_count = lax.axis_size("vir")
    blocks_dev = amplitudes.shape[0]
    slot_count = integrals.shape[0]
    capacity = max(2, 3 * blocks_dev // (2 * vir_count))
    vir_index = lax.axis_index("vir")
    owner_rank, src_rank = block_ranks(block_owner, blocks_dev)
    block_ids = jnp.arange(block_owner.shape[0], dtype=jnp.int32)
    is_mine = block_owner == vir_index
    slot_pick = is_mine[None, :] & (
        owner_rank[None, :] == jnp.arange(slot_count, dtype=jnp.int32)[:, None]
    )
    slot_live = jnp.sum(jnp.where(slot_pick, 1, 0), axis=1)
    chosen = jnp.sum(jnp.where(slot_pick, block_ids[None, :], 0), axis=1)
    flat_index = chosen // blocks_dev * capacity + src_rank[chosen]
    slot_mask = slot_live.astype(jnp.float32)[:, None, None]
    local_ids = vir_index * blocks_dev + jnp.arange(blocks_dev, dtype=jnp.int32)
    target = block_owner[local_ids]
    target_rank = src_rank[local_ids]
    target_hit = (
        target[None, None, :] == jnp.arange(vir_count, dtype=jnp.int32)[:, None, None]
    ) & (target_rank[None, None, :] == jnp.arange(capacity, dtype=jnp.int32)[None, :, None])
    send_index = jnp.sum(
        jnp.where(target_hit, jnp.arange(blocks_dev, dtype=jnp.int32)[None, None, :], 0), axis=2
    )
    send_live = jnp.sum(jnp.where(target_hit, 1, 0), axis=2).astype(jnp.float32)
    outgoing = jnp.take(amplitudes, send_index, axis=0) * send_live[:, :, None, None]
    arrived = lax.all_to_all(outgoing, "vir", split_axis=0, concat_axis=0, tiled=True)
    row_stack = arrived.reshape((arrived.shape[0] * arrived.shape[1],) + arrived.shape[2:])
    owned = jnp.take(row_stack, flat_index, axis=0) * slot_mask
    owned = lax.all_to_all(owned, ("occ", "rep"), split_axis=2, concat_axis=1, tiled=True)
    partial_value = contract(owned, integrals)
    rep_part = lax.psum_scatter(partial_value, "rep", scatter_dimension=1, tiled=True)
    pair_part = lax.psum_scatter(rep_part, "occ", scatter_dimension=0, tiled=True)
    return lax.psum(pair_part, "vir")


def solution(mesh):
    in_specs = (P("vir", ("occ", "rep"), None), P("vir", None, ("occ", "rep")), P())
    out_specs = P("occ", "rep")
    return jax.shard_map(
        on_device, mesh=mesh, in_specs=in_specs, out_specs=out_specs, check_vma=False
    )
```

profile of v0, /device:TPU:0, one launch (start us, length us, event | category | flops | bytes accessed | tf_op | source)
XLA Modules:
  0.0 531.7 jit_solution(18139110158587541731)
XLA Ops:
  6.5 0.0 copy-start
  6.6 1.0 select_reduce_fusion.1
  7.6 1.3 gather_fusion.1
  8.9 0.6 gather_fusion.2
  9.6 0.1 iota_compare_fusion.2
  9.7 0.1 fusion.8
  9.8 0.1 copy.20
  9.9 0.1 reshape.278
  10.0 0.1 copy.19
  10.1 0.1 copy.21
  10.2 0.0 copy-done
  10.2 4.3 gather_fusion.3
  14.5 8.5 %select_multiply_fusion = f32[32,2,8,4096]{3,2,1,0:T(8,128)} fusion(f32[32,2,8,4096]{3,2,1,0:T(8,128)} %bitcast.42, f32[32,2]{1,0:T(8,128)S(1)} %copy.21, pred[32,2]{1,0:T(8,128)(4,1)S(1)} %copy.19), kind=kLoop, calls=%fused_computation.5 | loop fusion | flops 4194304 | bytes 16777536 | tf_op jit(solution)/shard_map/mul | solution.py:55
  22.9 0.0 copy-start.2
  22.9 9.8 %all-to-all-start = ((f32[32,2,8,4096]{3,2,1,0:T(8,128)}), f32[32,2,8,4096]{3,2,1,0:T(8,128)}, u32[]{:S(2)}, u32[]{:S(2)}) async-start(f32[32,2,8,4096]{3,2,1,0:T(8,128)} %select_multiply_fusion), calls=%async_computation | async-start | bytes 16777216 | tf_op jit(solution)/shard_map/all_to_all | solution.py:56
  32.8 0.0 reduce-scatter.3.cloned.1.call-start
  32.8 0.0 copy-done.2
  32.9 0.1 select_reduce_fusion.2
  33.0 0.7 gather_fusion
  33.7 187.9 %all-to-all-done = f32[32,2,8,4096]{3,2,1,0:T(8,128)} async-done(((f32[32,2,8,4096]{3,2,1,0:T(8,128)}), f32[32,2,8,4096]{3,2,1,0:T(8,128)}, u32[]{:S(2)}, u32[]{:S(2)}) %all-to-all-start) | async-done | bytes 8388640 | tf_op jit(solution)/shard_map/all_to_all | solution.py:56
  221.6 5.3 gather_fusion.4
  226.9 1.6 select_multiply_fusion.1
  228.5 9.0 %copy.22 = f32[12,8,4096]{0,1,2:T(8,128)} copy(f32[12,8,4096]{2,1,0:T(8,128)S(1)} %select_multiply_fusion.1) | data formatting | bytes 3145728 | tf_op jit(solution)/shard_map/mul | solution.py:58
  237.5 18.2 %reshape.294 = f32[8,1,49152]{2,1,0:T(1,128)S(1)} reshape(f32[4096,8,12]{2,1,0:T(8,128)} %bitcast.40) | data formatting | bytes 3145728
  255.7 26.2 %all_to_all.23 = f32[8,1,49152]{2,1,0:T(1,128)} all-to-all(f32[8,1,49152]{2,1,0:T(1,128)S(1)} %reshape.294), channel_id=1, replica_groups=mesh['vir'=32,'occ'=4,'rep'=2] {'occ','rep'}, dimensions={0} | all-to-all | bytes 3145728 | tf_op jit(solution)/shard_map/all_to_all | solution.py:59
  281.9 0.5 broadcast.330
  282.4 5.8 %reduce = f32[8,49152]{1,0:T(8,128)S(1)} reduce(f32[8,1,49152]{2,1,0:T(1,128)} %all_to_all.23, f32[]{:T(128)} %broadcast.330), dimensions={1}, to_apply=%all_to_all.17.reduce_sub_computation | reduce | bytes 3145732 | tf_op jit(solution)/shard_map/all_to_all | solution.py:59
  288.2 24.4 %reshape.295 = f32[4096,8,12]{2,1,0:T(8,128)} reshape(f32[8,49152]{1,0:T(8,128)S(1)} %reduce) | data formatting | bytes 3145728
  312.6 0.0 copy-start.1
  312.6 10.2 %copy.23 = f32[12,8,8,512]{3,1,2,0:T(8,128)S(1)} copy(f32[12,8,8,512]{0,1,3,2:T(8,128)} %bitcast.41) | data formatting | bytes 3145728 | tf_op jit(solution)/shard_map/all_to_all | solution.py:59
  322.8 15.7 %fusion.2 = f32[64,512]{1,0:T(8,128)} fusion(f32[12,512,512]{2,1,0:T(8,128)} %param.4, f32[12,8,8,512]{3,1,2,0:T(8,128)S(1)} %copy.23), kind=kOutput, calls=%fused_computation.9 | convolution fusion | flops 2415919104 | bytes 14286848 | tf_op jit(solution)/shard_map/vpx,vax->pa/dot_general | solution.py:20
  338.5 0.0 reduce-scatter.3.cloned.1.call-update
  338.5 0.0 reduce-scatter.5.cloned.1.call-start
  338.6 16.5 %reduce-scatter.3.cloned.1.call-done = f32[64,256]{1,0:T(8,128)} async-done(((f32[64,512]{1,0:T(8,128)}), f32[64,256]{1,0:T(8,128)}) %reduce-scatter.3.cloned.1.call-update) | async-done | bytes 65552 | tf_op jit(solution)/shard_map/reduce_scatter | solution.py:61
  355.1 0.0 reduce-scatter.5.cloned.1.call-update
  355.1 26.6 %reduce-scatter.5.cloned.1.call-done = f32[16,256]{1,0:T(8,128)} async-done(((f32[64,256]{1,0:T(8,128)}), f32[16,256]{1,0:T(8,128)}) %reduce-scatter.5.cloned.1.call-update) | async-done | bytes 16400 | tf_op jit(solution)/shard_map/reduce_scatter | solution.py:62
  381.8 143.1 %psum.7 = f32[16,256]{1,0:T(8,128)} all-reduce(f32[16,256]{1,0:T(8,128)} %reduce-scatter.5.cloned.1.call-done), channel_id=1, replica_groups=mesh['vir'=32,'occ'=4,'rep'=2] {'vir'}, use_global_device_ids=true, to_apply=%region_8.9 | all-reduce | flops 4096 | bytes 32768 | tf_op jit(solution)/shard_map/psum | solution.py:63
  524.9 0.0 copy-done.1
  (15 shorter events, 0.1 us)
Async XLA Ops:
  6.5 3.6 copy-start
  22.9 9.9 %copy-start.2 = (s32[256]{0:T(256)S(1)}, s32[256]{0:T(256)}, u32[]{:S(2)}) copy-start(s32[256]{0:T(256)} %param.5) | copy-start | bytes 3076
  22.9 198.6 %all-to-all-start = ((f32[32,2,8,4096]{3,2,1,0:T(8,128)}), f32[32,2,8,4096]{3,2,1,0:T(8,128)}, u32[]{:S(2)}, u32[]{:S(2)}) async-start(f32[32,2,8,4096]{3,2,1,0:T(8,128)} %select_multiply_fusion), calls=%async_computation | async-start | bytes 16777216 | tf_op jit(solution)/shard_map/all_to_all | solution.py:56
  32.8 322.3 %reduce-scatter.3.cloned.1.call-start = ((), (), s32[]{:S(2)}) async-start(), calls=%async_computation.4 | async-start | bytes 196608 | tf_op jit(solution)/shard_map/reduce_scatter | solution.py:61
  312.6 212.3 %copy-start.1 = (f32[8,8,4096]{2,1,0:T(8,128)S(1)}, f32[8,8,4096]{2,1,0:T(8,128)}, u32[]{:S(2)}) copy-start(f32[8,8,4096]{2,1,0:T(8,128)} %param.3) | copy-start | bytes 3145732
  338.5 43.3 %reduce-scatter.5.cloned.1.call-start = ((), (), s32[]{:S(2)}) async-start(), calls=%async_computation.5 | async-start | bytes 81920 | tf_op jit(solution)/shard_map/reduce_scatter | solution.py:62
Sparse Core Ops, SparseCore 0:
  338.7 16.4 reduce-scatter.2
  357.6 24.1 reduce-scatter.4
where the time goes:
time: 532 us
  waiting for transfers between devices  231 us (43%)
  blocking collectives  169 us (32%)
  local copies, waits for them, and re-layouts  74.9 us (14%)
  other arithmetic  17.3 us (3%)
  matrix products  15.7 us (3%)
  between operations  13.5 us (3%)
  starting transfers between devices  9.92 us (2%)
    all_to_all x1, waiting for transfers between devices, on_device(): lax.all_to_all(outgoing, 'vir', split_axis=0, concat_axis=0, tiled=True)  188 us
    psum x1, blocking collectives, on_device(): return lax.psum(pair_part, 'vir')  143 us
    unnamed x8, local copies, waits for them, and re-layouts  42.6 us
    reduce_scatter x1, waiting for transfers between devices, on_device(): lax.psum_scatter(rep_part, 'occ', scatter_dimension=0, tiled=True)  26.6 us
    all_to_all x1, blocking collectives, on_device(): lax.all_to_all(owned, ('occ', 'rep'), split_axis=2, concat_axis=1, tiled=...  26.2 us
    reduce_scatter x1, waiting for transfers between devices, on_device(): lax.psum_scatter(partial_value, 'rep', scatter_dimension=1, tiled=True)  16.5 us
    dot_general x1, matrix products, contract(): jnp.einsum('vpx,vax->pa', owned, integrals, precision=lax.Precision.HIGHE...  15.7 us
    all_to_all x2, local copies, waits for them, and re-layouts, on_device(): lax.all_to_all(owned, ('occ', 'rep'), split_axis=2, concat_axis=1, tiled=...  10.7 us
  transfers between devices with their start and end apart: 3, of which 3 were waited for; matrix products, arithmetic and copies ran while one was open for 0% of the time, Pallas kernels for 0%

commit v1 on v0

--- a/solution.py
+++ b/solution.py
@@ -1,7 +1,33 @@
+import functools
 import jax
 import jax.numpy as jnp
 from jax import lax
 from jax.sharding import PartitionSpec as P
+
+
+def refer_the_corner(view, axis_tag, dimension_no, on_dim):
+    after, local_now = (lax.axis_size(axis_tag), lax.axis_index(axis_tag))
+    later = view.shape[dimension_no] // after
+    right_arr = jnp.roll(view, -local_now * later, axis=dimension_no)
+    kept_rows = [lax.slice_in_dim(right_arr, 0, later, axis=dimension_no)]
+    for t in tuple(range(1, after)):
+        arr_now = lax.slice_in_dim(right_arr, t * later, (t + 1) * later, axis=dimension_no)
+        kept_rows.append(
+            lax.ppermute(
+                arr_now, axis_name=axis_tag, perm=[(pp, (pp + t) % after) for pp in range(after)]
+            )
+        )
+    inter = jnp.roll(
+        jnp.concatenate(kept_rows[::-1], axis=on_dim),
+        (local_now + 1) * kept_rows[0].shape[on_dim],
+        axis=on_dim,
+    )
+    return inter
+
+
+_refer_corner = functools.partial(
+    refer_the_corner, axis_tag=("occ", "rep"), dimension_no=2, on_dim=1
+)
 
 
 def block_ranks(owners, blocks_dev):
@@ -56,7 +82,7 @@
     arrived = lax.all_to_all(outgoing, "vir", split_axis=0, concat_axis=0, tiled=True)
     row_stack = arrived.reshape((arrived.shape[0] * arrived.shape[1],) + arrived.shape[2:])
     owned = jnp.take(row_stack, flat_index, axis=0) * slot_mask
-    owned = lax.all_to_all(owned, ("occ", "rep"), split_axis=2, concat_axis=1, tiled=True)
+    owned = _refer_corner(owned)
     partial_value = contract(owned, integrals)
     rep_part = lax.psum_scatter(partial_value, "rep", scatter_dimension=1, tiled=True)
     pair_part = lax.psum_scatter(rep_part, "occ", scatter_dimension=0, tiled=True)

time: 532 us -> 461 us (0.87)
  local copies, waits for them, and re-layouts: 74.9 us -> 12.6 us
  blocking collectives: 169 us -> 143 us
  waiting for transfers between devices: 231 us -> 248 us
  starting transfers between devices: 9.92 us -> 17.1 us
  other arithmetic: 17.3 us -> 10.4 us
    unnamed x8 -> x19, local copies, waits for them, and re-layouts: 42.6 us -> 0.23 us
    all_to_all x1 -> x0, blocking collectives: 26.2 us -> none  [on_device(): lax.all_to_all(owned, ('occ', 'rep'), split_axis=2, concat_axis=1, tiled=...]
    ppermute x0 -> x7, waiting for transfers between devices: none -> 17.7 us  [refer_the_corner(): lax.ppermute(arr_now, axis_name=axis_tag, perm=[(pp, (pp + t) % after) fo...]
    all_to_all x2 -> x0, local copies, waits for them, and re-layouts: 10.7 us -> none  [on_device(): lax.all_to_all(owned, ('occ', 'rep'), split_axis=2, concat_axis=1, tiled=...]
    mul x1 -> x0, local copies, waits for them, and re-layouts: 9.02 us -> none  [on_device(): owned = jnp.take(row_stack, flat_index, axis=0) * slot_mask]
    ppermute x0 -> x7, starting transfers between devices: none -> 7.19 us  [refer_the_corner(): lax.ppermute(arr_now, axis_name=axis_tag, perm=[(pp, (pp + t) % after) fo...]
    all_to_all x1 -> x0, other arithmetic: 5.79 us -> none  [on_device(): lax.all_to_all(owned, ('occ', 'rep'), split_axis=2, concat_axis=1, tiled=...]
  transfers between devices with their start and end apart: 3 -> 10, of which waited for: 3 -> 8; matrix products, arithmetic and copies ran while one was open for 0% -> 0% of each run, Pallas kernels for 0% -> 0%
where the time goes in v1:
time: 461 us
  waiting for transfers between devices  248 us (54%)
  blocking collectives  143 us (31%)
  starting transfers between devices  17.1 us (4%)
  matrix products  15.7 us (3%)
  between operations  13.7 us (3%)
  local copies, waits for them, and re-layouts  12.6 us (3%)
  other arithmetic  10.4 us (2%)
    all_to_all x1, waiting for transfers between devices, on_device(): lax.all_to_all(outgoing, 'vir', split_axis=0, concat_axis=0, tiled=True)  188 us
    psum x1, blocking collectives, on_device(): return lax.psum(pair_part, 'vir')  143 us
    reduce_scatter x1, waiting for transfers between devices, on_device(): lax.psum_scatter(rep_part, 'occ', scatter_dimension=0, tiled=True)  26.6 us
    ppermute x7, waiting for transfers between devices, refer_the_corner(): lax.ppermute(arr_now, axis_name=axis_tag, perm=[(pp, (pp + t) % after) fo...  17.7 us
    reduce_scatter x1, waiting for transfers between devices, on_device(): lax.psum_scatter(partial_value, 'rep', scatter_dimension=1, tiled=True)  16 us
    dot_general x1, matrix products, contract(): jnp.einsum('vpx,vax->pa', owned, integrals, precision=lax.Precision.HIGHE...  15.7 us
    all_to_all x1, starting transfers between devices, on_device(): lax.all_to_all(outgoing, 'vir', split_axis=0, concat_axis=0, tiled=True)  9.84 us
  transfers between devices with their start and end apart: 10, of which 8 were waited for; matrix products, arithmetic and copies ran while one was open for 0% of the time, Pallas kernels for 0%

profile of v1, /device:TPU:0, one launch (start us, length us, event | category | flops | bytes accessed | tf_op | source)
XLA Modules:
  0.0 460.8 jit_solution(3068517954660464515)
XLA Ops:
  6.5 0.0 copy-start
  6.6 1.0 select_reduce_fusion.1
  7.6 1.3 gather_fusion.1
  8.9 0.6 gather_fusion.2
  9.6 0.1 iota_compare_fusion.2
  9.7 0.1 fusion.9
  9.8 0.1 copy.9
  9.9 0.1 reshape.278
  10.0 0.1 copy.8
  10.1 0.1 copy.10
  10.2 0.0 copy-done
  10.2 4.3 gather_fusion.3
  14.5 8.5 %select_multiply_fusion = f32[32,2,8,4096]{3,2,1,0:T(8,128)} fusion(f32[32,2,8,4096]{3,2,1,0:T(8,128)} %bitcast.30, f32[32,2]{1,0:T(8,128)S(1)} %copy.10, pred[32,2]{1,0:T(8,128)(4,1)S(1)} %copy.8), kind=kLoop, calls=%fused_computation.5 | loop fusion | flops 4194304 | bytes 16777536 | tf_op jit(solution)/shard_map/mul | solution.py:81
  22.9 0.0 copy-start.1
  22.9 9.8 %all-to-all-start = ((f32[32,2,8,4096]{3,2,1,0:T(8,128)}), f32[32,2,8,4096]{3,2,1,0:T(8,128)}, u32[]{:S(2)}, u32[]{:S(2)}) async-start(f32[32,2,8,4096]{3,2,1,0:T(8,128)} %select_multiply_fusion), calls=%async_computation | async-start | bytes 16777216 | tf_op jit(solution)/shard_map/all_to_all | solution.py:82
  32.8 0.0 reduce-scatter.3.cloned.1.call-start
  32.9 0.0 copy-done.1
  32.9 0.1 select_reduce_fusion.2
  33.0 0.7 gather_fusion
  33.8 187.8 %all-to-all-done = f32[32,2,8,4096]{3,2,1,0:T(8,128)} async-done(((f32[32,2,8,4096]{3,2,1,0:T(8,128)}), f32[32,2,8,4096]{3,2,1,0:T(8,128)}, u32[]{:S(2)}, u32[]{:S(2)}) %all-to-all-start) | async-done | bytes 8388640 | tf_op jit(solution)/shard_map/all_to_all | solution.py:82
  221.6 4.0 gather_fusion.4
  225.6 0.2 select_multiply_fusion.1
  225.8 0.3 fusion
  226.2 1.0 fusion.14
  227.2 1.6 collective-permute-start
  228.7 1.4 collective-permute-start.1
  230.2 0.5 collective-permute-start.2
  230.6 2.9 collective-permute-start.3
  233.5 0.0 collective-permute-start.4
  233.5 0.0 collective-permute-done
  233.5 0.8 collective-permute-start.5
  234.4 4.5 collective-permute-done.1
  238.9 0.0 collective-permute-start.6
  238.9 0.0 collective-permute-done.2
  239.0 4.8 %collective-permute-done.3 = f32[12,8,512]{2,1,0:T(8,128)S(1)} collective-permute-done((f32[12,8,512]{2,1,0:T(8,128)}, f32[12,8,512]{2,1,0:T(8,128)S(1)}, u32[]{:S(2)}, u32[]{:S(2)}) %collective-permute-start.3) | collective-permute-done | bytes 196640 | tf_op jit(solution)/shard_map/ppermute | solution.py:16
  243.7 0.1 collective-permute-done.4
  243.9 8.2 %collective-permute-done.5 = f32[12,8,512]{2,1,0:T(8,128)S(1)} collective-permute-done((f32[12,8,512]{2,1,0:T(8,128)S(1)}, f32[12,8,512]{2,1,0:T(8,128)S(1)}, u32[]{:S(2)}, u32[]{:S(2)}) %collective-permute-start.5) | collective-permute-done | bytes 196640 | tf_op jit(solution)/shard_map/ppermute | solution.py:16
  252.1 0.1 collective-permute-done.6
  252.4 15.7 %fusion.3 = f32[64,512]{1,0:T(8,128)} fusion(f32[12,512,512]{2,1,0:T(8,128)} %param.4, f32[12,128,512]{2,1,0:T(8,128)S(1)} %slice_dynamic-update-slice_fusion.1, s32[]{:T(128)S(6)} %select_n.160), kind=kOutput, calls=%fused_computation.12 | convolution fusion | flops 2415919104 | bytes 14286852 | tf_op jit(solution)/shard_map/vpx,vax->pa/dot_general | solution.py:46
  268.1 0.0 reduce-scatter.3.cloned.1.call-update
  268.1 0.0 reduce-scatter.5.cloned.1.call-start
  268.2 16.0 %reduce-scatter.3.cloned.1.call-done = f32[64,256]{1,0:T(8,128)} async-done(((f32[64,512]{1,0:T(8,128)}), f32[64,256]{1,0:T(8,128)}) %reduce-scatter.3.cloned.1.call-update) | async-done | bytes 65552 | tf_op jit(solution)/shard_map/reduce_scatter | solution.py:87
  284.2 0.0 reduce-scatter.5.cloned.1.call-update
  284.2 26.6 %reduce-scatter.5.cloned.1.call-done = f32[16,256]{1,0:T(8,128)} async-done(((f32[64,256]{1,0:T(8,128)}), f32[16,256]{1,0:T(8,128)}) %reduce-scatter.5.cloned.1.call-update) | async-done | bytes 16400 | tf_op jit(solution)/shard_map/reduce_scatter | solution.py:88
  310.8 143.1 %psum.7 = f32[16,256]{1,0:T(8,128)} all-reduce(f32[16,256]{1,0:T(8,128)} %reduce-scatter.5.cloned.1.call-done), channel_id=1, replica_groups=mesh['vir'=32,'occ'=4,'rep'=2] {'vir'}, use_global_device_ids=true, to_apply=%region_8.9 | all-reduce | flops 4096 | bytes 32768 | tf_op jit(solution)/shard_map/psum | solution.py:89
  (31 shorter events, 0.4 us)
Async XLA Ops:
  6.5 3.6 copy-start
  22.9 9.9 %copy-start.1 = (s32[256]{0:T(256)S(1)}, s32[256]{0:T(256)}, u32[]{:S(2)}) copy-start(s32[256]{0:T(256)} %param.5) | copy-start | bytes 3076
  22.9 198.6 %all-to-all-start = ((f32[32,2,8,4096]{3,2,1,0:T(8,128)}), f32[32,2,8,4096]{3,2,1,0:T(8,128)}, u32[]{:S(2)}, u32[]{:S(2)}) async-start(f32[32,2,8,4096]{3,2,1,0:T(8,128)} %select_multiply_fusion), calls=%async_computation | async-start | bytes 16777216 | tf_op jit(solution)/shard_map/all_to_all | solution.py:82
  32.8 251.4 %reduce-scatter.3.cloned.1.call-start = ((), (), s32[]{:S(2)}) async-start(), calls=%async_computation.3 | async-start | bytes 196608 | tf_op jit(solution)/shard_map/reduce_scatter | solution.py:87
  227.2 6.4 %collective-permute-start = (f32[12,8,512]{2,1,0:T(8,128)}, f32[12,8,512]{2,1,0:T(8,128)S(1)}, u32[]{:S(2)}, u32[]{:S(2)}) collective-permute-start(f32[12,8,512]{2,1,0:T(8,128)} %get-tuple-element.17), channel_id=1, source_target_pairs={{0,7},{1,0},{2,1},{3,2},{4,3},{5,4},{6,5},{7,6},{8,15},{9,8},{10,9... | collective-permute-start | bytes 589832 | tf_op jit(solution)/shard_map/ppermute | solution.py:16
  228.7 10.2 %collective-permute-start.1 = (f32[12,8,512]{2,1,0:T(8,128)}, f32[12,8,512]{2,1,0:T(8,128)S(1)}, u32[]{:S(2)}, u32[]{:S(2)}) collective-permute-start(f32[12,8,512]{2,1,0:T(8,128)} %get-tuple-element.16), channel_id=1, source_target_pairs={{0,6},{1,7},{2,0},{3,1},{4,2},{5,3},{6,4},{7,5},{8,14},{9,15},{10,... | collective-permute-start | bytes 589832 | tf_op jit(solution)/shard_map/ppermute | solution.py:16
  230.2 8.8 %collective-permute-start.2 = (f32[12,8,512]{2,1,0:T(8,128)}, f32[12,8,512]{2,1,0:T(8,128)S(1)}, u32[]{:S(2)}, u32[]{:S(2)}) collective-permute-start(f32[12,8,512]{2,1,0:T(8,128)} %get-tuple-element.15), channel_id=1, source_target_pairs={{0,5},{1,6},{2,7},{3,0},{4,1},{5,2},{6,3},{7,4},{8,13},{9,14},{10,... | collective-permute-start | bytes 589832 | tf_op jit(solution)/shard_map/ppermute | solution.py:16
  230.6 13.1 %collective-permute-start.3 = (f32[12,8,512]{2,1,0:T(8,128)}, f32[12,8,512]{2,1,0:T(8,128)S(1)}, u32[]{:S(2)}, u32[]{:S(2)}) collective-permute-start(f32[12,8,512]{2,1,0:T(8,128)} %get-tuple-element.14), channel_id=1, source_target_pairs={{0,4},{1,5},{2,6},{3,7},{4,0},{5,1},{6,2},{7,3},{8,12},{9,13},{10,... | collective-permute-start | bytes 589832 | tf_op jit(solution)/shard_map/ppermute | solution.py:16
  233.5 10.3 %collective-permute-start.4 = (f32[12,8,512]{2,1,0:T(8,128)}, f32[12,8,512]{2,1,0:T(8,128)S(1)}, u32[]{:S(2)}, u32[]{:S(2)}) collective-permute-start(f32[12,8,512]{2,1,0:T(8,128)} %get-tuple-element.13), channel_id=1, source_target_pairs={{0,3},{1,4},{2,5},{3,6},{4,7},{5,0},{6,1},{7,2},{8,11},{9,12},{10,... | collective-permute-start | bytes 589832 | tf_op jit(solution)/shard_map/ppermute | solution.py:16
  233.5 18.5 %collective-permute-start.5 = (f32[12,8,512]{2,1,0:T(8,128)S(1)}, f32[12,8,512]{2,1,0:T(8,128)S(1)}, u32[]{:S(2)}, u32[]{:S(2)}) collective-permute-start(f32[12,8,512]{2,1,0:T(8,128)S(1)} %get-tuple-element.12), channel_id=1, source_target_pairs={{0,2},{1,3},{2,4},{3,5},{4,6},{5,7},{6,0},{7,1},{8,10},{9,11},{10,... | collective-permute-start | bytes 589832 | tf_op jit(solution)/shard_map/ppermute | solution.py:16
  238.9 13.2 %collective-permute-start.6 = (f32[12,8,512]{2,1,0:T(8,128)S(1)}, f32[12,8,512]{2,1,0:T(8,128)S(1)}, u32[]{:S(2)}, u32[]{:S(2)}) collective-permute-start(f32[12,8,512]{2,1,0:T(8,128)S(1)} %get-tuple-element.11), channel_id=1, source_target_pairs={{0,1},{1,2},{2,3},{3,4},{4,5},{5,6},{6,7},{7,0},{8,9},{9,10},{10,1... | collective-permute-start | bytes 589832 | tf_op jit(solution)/shard_map/ppermute | solution.py:16
  268.1 42.7 %reduce-scatter.5.cloned.1.call-start = ((), (), s32[]{:S(2)}) async-start(), calls=%async_computation.4 | async-start | bytes 81920 | tf_op jit(solution)/shard_map/reduce_scatter | solution.py:88
Sparse Core Ops, SparseCore 0:
  268.2 15.8 reduce-scatter.2
  286.7 24.1 reduce-scatter.4
